TPU v7x, 32 devices: a whole 2x2x4 slice. The times are simulated.
32 devices in a mesh: ex: 8 (over z, x), tp: 4 (over y, core).
Axes of the slice: x: 2, y: 2, z: 4, core: 2. Of those that a mesh axis runs over, the one named last changes fastest.
Arguments:
- inputs: bfloat16 [1024, 768], P('ex'), may hold values from -6 to 6
- routes: int32 [1024, 2], P('ex'), may hold values from 0 to 7, all different within a row; in each aligned block of 128 rows (0 to 127, 128 to 255, ...) at most 64 rows name the same one
- lengths: int32 [8, 4], P('ex'), may hold values from 1 to 96, 128 in all within a row
- w_query: bfloat16 [768, 768], P(None, 'tp'), may hold values from -0.21875 to 0.21875
- w_key: bfloat16 [768, 768], P(None, 'tp'), may hold values from -0.21875 to 0.21875
- w_value: bfloat16 [768, 768], P(None, 'tp'), may hold values from -0.21875 to 0.21875
- w_attn_out: bfloat16 [768, 768], P('tp'), may hold values from -0.875 to 0.875
- gain_attn: float32 [768], replicated, may hold values from 0.25 to 1.75
- gain_moe: float32 [768], replicated, may hold values from 0.25 to 1.75
- rel_bias: float32 [32, 12], P(None, 'tp'), may hold values from -4 to 4
- w_router: bfloat16 [768, 8], replicated, may hold values from -0.15625 to 0.15625
- w_in: bfloat16 [8, 768, 3072], P('ex', None, 'tp'), may hold values from -0.21875 to 0.21875
- w_out: bfloat16 [8, 3072, 768], P('ex', 'tp'), may hold values from -0.109375 to 0.109375
- cotangent: bfloat16 [1024, 768], P('ex'), may hold values from -6 to 6
Outputs:
- output: bfloat16 [1024, 768], P('ex')
- grad_inputs: bfloat16 [1024, 768], P('ex')
- grad_w_query: float32 [768, 768], P(None, 'tp')
- grad_w_key: float32 [768, 768], P(None, 'tp')
- grad_w_value: float32 [768, 768], P(None, 'tp')
- grad_w_attn_out: float32 [768, 768], P('tp')
- grad_gain_attn: float32 [768], replicated
- grad_gain_moe: float32 [768], replicated
- grad_rel_bias: float32 [32, 12], P(None, 'tp')
- grad_w_router: float32 [768, 8], replicated
- grad_w_in: float32 [8, 768, 3072], P('ex', None, 'tp')
- grad_w_out: float32 [8, 3072, 768], P('ex', 'tp')
Inputs may be any that keep to these rules, and one draw needn't show every extreme that they name: `routes`: each row names two different experts. The rows of one index of ex name any one expert at most 64 times, a bound that some block reaches. `lengths`: each row sums to 128 and its largest entry is exactly 96.
All inputs are finite; a program needn't handle non-finite values.
Results may differ from a plain program's by a relative error of at most 0.017.
Values may be sent and summed in bfloat16 or wider, within the bound.
A program may use at most 128 MiB of HBM per device.

v0:
```python
from functools import partial
import math
import jax
import jax.numpy as jnp
from jax import lax
from jax.sharding import PartitionSpec as P

eps = 1e-06
highest = lax.Precision.HIGHEST
bucket_edges = [math.ceil(16 * 8 ** (number / 16)) for number in range(1, 16)]


def rms_scale(values):
    return lax.rsqrt(jnp.mean(values * values, -1, keepdims=True) + eps)


def bucket_of(length):
    positions = jnp.arange(length, dtype=jnp.int32)
    offsets = positions[:, None] - positions[None, :]
    distance = jnp.maximum(offsets, 0)
    counted = jnp.zeros_like(distance)
    for border in bucket_edges:
        counted = counted + (distance >= border).astype(jnp.int32)
    return jnp.where(distance < 16, distance, 16 + counted)


def contract_rows(left_side, right_side):
    return lax.dot_general(
        left_side, right_side, (((0,), (0,)), ((), ())), preferred_element_type=jnp.float32
    )


def contract_cols(left_side, right_side):
    return lax.dot_general(
        left_side, right_side, (((1,), (1,)), ((), ())), preferred_element_type=jnp.float32
    )


def shards(
    inputs,
    routes,
    lengths,
    w_query,
    w_key,
    w_value,
    w_attn_out,
    gain_attn,
    gain_moe,
    rel_bias,
    w_router,
    w_in,
    w_out,
    cotangent,
):
    tok_rows, model_width = inputs.shape
    local_heads = rel_bias.shape[1]
    head_dim = w_query.shape[1] // local_heads
    attn_scale = head_dim ** (-0.5)
    experts = w_router.shape[1]
    ex_devices = lax.axis_size("ex")
    local_experts = w_in.shape[0]
    capacity = 4 * tok_rows // experts
    pair_count = 2 * tok_rows
    inputs_f = inputs.astype(jnp.float32)
    scale_a = rms_scale(inputs_f)
    normed_a = inputs_f * scale_a
    attn_in = (normed_a * gain_attn).astype(jnp.bfloat16)
    query_b = (
        jnp.dot(attn_in, w_query, preferred_element_type=jnp.float32)
        .astype(jnp.bfloat16)
        .reshape(tok_rows, local_heads, head_dim)
    )
    key_b = (
        jnp.dot(attn_in, w_key, preferred_element_type=jnp.float32)
        .astype(jnp.bfloat16)
        .reshape(tok_rows, local_heads, head_dim)
    )
    value_b = (
        jnp.dot(attn_in, w_value, preferred_element_type=jnp.float32)
        .astype(jnp.bfloat16)
        .reshape(tok_rows, local_heads, head_dim)
    )
    buckets = bucket_of(tok_rows)
    one_hot = (
        buckets[None] == jnp.arange(rel_bias.shape[0], dtype=jnp.int32)[:, None, None]
    ).astype(jnp.float32)
    bias_full = jnp.einsum("bij,bh->hij", one_hot, rel_bias, precision=highest)
    seq_count = lengths.shape[1]
    seq_order = jnp.arange(seq_count, dtype=jnp.int32)
    seq_ends = jnp.sum(
        jnp.where(seq_order[None, :] <= seq_order[:, None], lengths[0][None, :], 0), -1
    )
    positions = jnp.arange(tok_rows, dtype=jnp.int32)
    segments = jnp.sum((positions[:, None] >= seq_ends[None, :]).astype(jnp.int32), -1)
    allowed = (segments[:, None] == segments[None, :]) & (positions[:, None] >= positions[None, :])

    def score_of(queries_in, keys_in):
        raw_scores = (
            jnp.einsum("ihd,jhd->hij", queries_in, keys_in, preferred_element_type=jnp.float32)
            * attn_scale
        )
        return jnp.where(allowed[None], raw_scores + bias_full, -1e30)

    scores = score_of(query_b, key_b)
    row_max = jnp.max(scores, -1, keepdims=True)
    log_sum = row_max + jnp.log(jnp.sum(jnp.exp(scores - row_max), -1, keepdims=True))
    probabilities = jnp.exp(scores - log_sum)
    probs_low = probabilities.astype(jnp.bfloat16)
    mixed_heads = (
        jnp.einsum("hij,jhd->ihd", probs_low, value_b, preferred_element_type=jnp.float32)
        .astype(jnp.bfloat16)
        .reshape(tok_rows, -1)
    )
    head_part = jnp.dot(mixed_heads, w_attn_out, preferred_element_type=jnp.float32)
    residual = inputs_f + lax.psum(head_part, "tp")
    scale_m = rms_scale(residual)
    normed_m = residual * scale_m
    moe_in = (normed_m * gain_moe).astype(jnp.bfloat16)
    logits = jnp.dot(moe_in, w_router, preferred_element_type=jnp.float32)
    expert_ids = jnp.arange(experts, dtype=jnp.int32)
    route_hot = (routes[:, :, None] == expert_ids[None, None, :]).astype(jnp.float32)
    chosen_logits = jnp.sum(route_hot * logits[:, None, :], -1)
    gate_max = jnp.max(chosen_logits, -1, keepdims=True)
    gate_exp = jnp.exp(chosen_logits - gate_max)
    gate_values = gate_exp / jnp.sum(gate_exp, -1, keepdims=True)
    pair_routes = routes.reshape(-1)
    pair_hot = (pair_routes[:, None] == expert_ids[None, :]).astype(jnp.int32)
    pair_order = jnp.arange(pair_count, dtype=jnp.int32)
    slot_index = jnp.sum(
        (
            (pair_routes[:, None] == pair_routes[None, :])
            & (pair_order[None, :] < pair_order[:, None])
        ).astype(jnp.int32),
        -1,
    )
    pair_slots = pair_routes * capacity + slot_index
    members = (
        jnp.full((experts * capacity,), pair_count, jnp.int32)
        .at[pair_slots]
        .set(jnp.arange(pair_count, dtype=jnp.int32))
    )
    padded = jnp.concatenate([moe_in, jnp.zeros((1, model_width), jnp.bfloat16)], 0)
    send_rows = padded[members // 2].reshape(experts, capacity, model_width)
    arrived = lax.all_to_all(send_rows, "ex", split_axis=0, concat_axis=0, tiled=True)
    slot_count = arrived.shape[1]
    grouped = arrived.reshape(ex_devices, local_experts, slot_count, model_width)
    pre_act = jnp.einsum("slcd,ldf->slcf", grouped, w_in, preferred_element_type=jnp.float32)
    act_low = jax.nn.gelu(pre_act, approximate=True).astype(jnp.bfloat16)
    partial_out = jnp.einsum("slcf,lfd->slcd", act_low, w_out, preferred_element_type=jnp.float32)
    partial_out = partial_out.reshape(ex_devices * local_experts, slot_count, model_width)
    owned_rows = lax.psum_scatter(
        partial_out.astype(jnp.bfloat16), "tp", scatter_dimension=2, tiled=True
    )
    returned = lax.all_to_all(owned_rows, "ex", split_axis=0, concat_axis=0, tiled=True)
    returned, kept_rows, kept_pre = (
        returned,
        arrived,
        pre_act.reshape(ex_devices * local_experts, slot_count, -1),
    )
    expert_out = lax.all_gather(returned, "tp", axis=2, tiled=True).reshape(
        experts * capacity, model_width
    )
    pair_out = expert_out[pair_slots].reshape(tok_rows, 2, model_width).astype(jnp.float32)
    result = residual + jnp.sum(gate_values[:, :, None] * pair_out, 1)
    output = result.astype(jnp.bfloat16)
    grad_out = cotangent.astype(jnp.float32)
    gate_grad = jnp.sum(grad_out[:, None, :] * pair_out, -1)
    logit_pair = gate_values * (gate_grad - jnp.sum(gate_values * gate_grad, -1, keepdims=True))
    logit_grads = jnp.sum(logit_pair[:, :, None] * route_hot, 1)
    grad_router = jnp.dot(moe_in.astype(jnp.float32).T, logit_grads, precision=highest)
    moe_grad = jnp.dot(logit_grads, w_router.astype(jnp.float32).T, precision=highest)
    pair_grads = (
        (gate_values[:, :, None] * grad_out[:, None, :])
        .astype(jnp.bfloat16)
        .reshape(pair_count, model_width)
    )
    padded_grads = jnp.concatenate([pair_grads, jnp.zeros((1, model_width), jnp.bfloat16)], 0)
    send_grad_rows = padded_grads[members].reshape(experts, capacity, model_width)
    arrived_grads = lax.all_to_all(send_grad_rows, "ex", split_axis=0, concat_axis=0, tiled=True)
    grad_group = arrived_grads.reshape(ex_devices, local_experts, capacity, model_width)
    act_grad = jnp.einsum("slcd,lfd->slcf", grad_group, w_out, preferred_element_type=jnp.float32)
    pre_keep = kept_pre.reshape(ex_devices, local_experts, capacity, -1)
    act_value, gelu_back = jax.vjp(partial(jax.nn.gelu, approximate=True), pre_keep)
    pre_grad = gelu_back(act_grad)[0].astype(jnp.bfloat16)
    act_low = act_value.astype(jnp.bfloat16)
    grad_w_out = jnp.einsum(
        "slcf,slcd->lfd", act_low, grad_group, preferred_element_type=jnp.float32
    )
    rows_group = kept_rows.reshape(ex_devices, local_experts, capacity, model_width)
    grad_w_in = jnp.einsum(
        "slcd,slcf->ldf", rows_group, pre_grad, preferred_element_type=jnp.float32
    )
    row_part = jnp.einsum("slcf,ldf->slcd", pre_grad, w_in, preferred_element_type=jnp.float32)
    row_part = row_part.reshape(ex_devices * local_experts, capacity, model_width)
    row_share = lax.psum_scatter(row_part, "tp", scatter_dimension=2, tiled=True).astype(
        jnp.bfloat16
    )
    row_back = lax.all_to_all(row_share, "ex", split_axis=0, concat_axis=0, tiled=True)
    row_full = lax.all_gather(row_back, "tp", axis=2, tiled=True).reshape(
        experts * capacity, model_width
    )
    moe_grad = moe_grad + jnp.sum(
        row_full[pair_slots].reshape(tok_rows, 2, model_width).astype(jnp.float32), 1
    )
    grad_gain_moe = jnp.sum(moe_grad * normed_m, 0)
    normed_grad_m = moe_grad * gain_moe
    resid_grad = grad_out + scale_m * (
        normed_grad_m - normed_m * jnp.mean(normed_grad_m * normed_m, -1, keepdims=True)
    )
    attn_grad = resid_grad.astype(jnp.bfloat16)
    grad_w_attn_out = contract_rows(mixed_heads, attn_grad)
    mixed_grad = (
        contract_cols(attn_grad, w_attn_out)
        .astype(jnp.bfloat16)
        .reshape(tok_rows, local_heads, head_dim)
    )
    scores_again = score_of(query_b, key_b)
    probs_again = jnp.exp(scores_again - log_sum)
    prob_grad = jnp.einsum("ihd,jhd->hij", mixed_grad, value_b, preferred_element_type=jnp.float32)
    value_grad = jnp.einsum(
        "hij,ihd->jhd",
        probs_again.astype(jnp.bfloat16),
        mixed_grad,
        preferred_element_type=jnp.float32,
    ).astype(jnp.bfloat16)
    score_grad = probs_again * (prob_grad - jnp.sum(probs_again * prob_grad, -1, keepdims=True))
    grad_rel_bias = jnp.einsum("hij,bij->bh", score_grad, one_hot, precision=highest)
    score_low = score_grad.astype(jnp.bfloat16)
    query_grad = (
        (
            jnp.einsum("hij,jhd->ihd", score_low, key_b, preferred_element_type=jnp.float32)
            * attn_scale
        )
        .astype(jnp.bfloat16)
        .reshape(tok_rows, -1)
    )
    key_grad = (
        (
            jnp.einsum("hij,ihd->jhd", score_low, query_b, preferred_element_type=jnp.float32)
            * attn_scale
        )
        .astype(jnp.bfloat16)
        .reshape(tok_rows, -1)
    )
    value_flat = value_grad.reshape(tok_rows, -1)
    grad_w_query = contract_rows(attn_in, query_grad)
    grad_w_key = contract_rows(attn_in, key_grad)
    grad_w_value = contract_rows(attn_in, value_flat)
    input_part = (
        contract_cols(query_grad, w_query)
        + contract_cols(key_grad, w_key)
        + contract_cols(value_flat, w_value)
    )
    input_grad = lax.psum(input_part.astype(jnp.bfloat16), "tp").astype(jnp.float32)
    grad_gain_attn = jnp.sum(input_grad * normed_a, 0)
    normed_grad_a = input_grad * gain_attn
    grad_inputs = (
        resid_grad
        + scale_a
        * (normed_grad_a - normed_a * jnp.mean(normed_grad_a * normed_a, -1, keepdims=True))
    ).astype(jnp.bfloat16)
    dense_sums = lax.psum(
        (
            grad_w_query,
            grad_w_key,
            grad_w_value,
            grad_w_attn_out,
            grad_gain_attn,
            grad_gain_moe,
            grad_rel_bias,
            grad_router,
        ),
        "ex",
    )
    return (
        output,
        grad_inputs,
        dense_sums[0],
        dense_sums[1],
        dense_sums[2],
        dense_sums[3],
        dense_sums[4],
        dense_sums[5],
        dense_sums[6],
        dense_sums[7],
        grad_w_in,
        grad_w_out,
    )


def solution(mesh):
    placed = (
        P("ex", None),
        P("ex", None),
        P("ex", None),
        P(None, "tp"),
        P(None, "tp"),
        P(None, "tp"),
        P("tp", None),
        P(),
        P(),
        P(None, "tp"),
        P(),
        P("ex", None, "tp"),
        P("ex", "tp", None),
        P("ex", None),
    )
    return jax.shard_map(
        shards,
        mesh=mesh,
        in_specs=placed,
        out_specs=(
            P("ex", None),
            P("ex", None),
            P(None, "tp"),
            P(None, "tp"),
            P(None, "tp"),
            P("tp", None),
            P(),
            P(),
            P(None, "tp"),
            P(),
            P("ex", None, "tp"),
            P("ex", "tp", None),
        ),
        check_vma=False,
    )
```

profile of v0, /device:TPU:0, one launch (start us, length us, event | category | flops | bytes accessed | tf_op | source)
XLA Modules:
  0.0 362.4 jit_solution(8996711575034821394)
XLA Ops:
  7.4 1.2 fusion.41
  8.7 1.4 fusion.1
  10.3 1.4 convolution_convert_fusion.6
  15.6 1.4 scatter_custom_fusion
  17.6 32.7 %all-reduce.8.cloned.1.call-done = f32[128,768]{1,0:T(8,128)} async-done(((f32[128,768]{1,0:T(8,128)}), f32[128,768]{1,0:T(8,128)}) %all-reduce.8.cloned.1.call-update) | async-done | bytes 393232 | tf_op jit(solution)/shard_map/psum | solution.py:115
  50.4 1.1 multiply_reduce_fusion.4
  52.8 2.7 gather_fusion
  55.5 5.6 %all-to-all-start = ((bf16[8,64,768]{2,1,0:T(8,128)(2,1)}), bf16[8,64,768]{2,1,0:T(8,128)(2,1)}, u32[]{:S(2)}, u32[]{:S(2)}) async-start(bf16[8,64,768]{2,1,0:T(8,128)(2,1)} %bitcast.10), calls=%async_computation | async-start | bytes 1572864 | tf_op jit(solution)/shard_map/all_to_all | solution.py:144
  65.3 2.7 gather_fusion.2
  68.0 12.4 %all-to-all-done = bf16[8,64,768]{2,1,0:T(8,128)(2,1)} async-done(((bf16[8,64,768]{2,1,0:T(8,128)(2,1)}), bf16[8,64,768]{2,1,0:T(8,128)(2,1)}, u32[]{:S(2)}, u32[]{:S(2)}) %all-to-all-start) | async-done | bytes 786464 | tf_op jit(solution)/shard_map/all_to_all | solution.py:144
  80.4 4.4 %all-to-all-start.2 = ((bf16[8,64,768]{2,1,0:T(8,128)(2,1)}), bf16[8,64,768]{2,1,0:T(8,128)(2,1)}, u32[]{:S(2)}, u32[]{:S(2)}) async-start(bf16[8,64,768]{2,1,0:T(8,128)(2,1)} %bitcast.22), calls=%async_computation.2 | async-start | bytes 1572864 | tf_op jit(solution)/shard_map/all_to_all | solution.py:179
  84.9 1.9 fusion.18
  86.8 1.1 copy-done.46
  87.9 2.0 convolution_convert_fusion
  89.9 2.0 copy.92
  91.9 1.7 reshape.444
  93.8 10.5 %all-to-all-done.2 = bf16[8,64,768]{2,1,0:T(8,128)(2,1)} async-done(((bf16[8,64,768]{2,1,0:T(8,128)(2,1)}), bf16[8,64,768]{2,1,0:T(8,128)(2,1)}, u32[]{:S(2)}, u32[]{:S(2)}) %all-to-all-start.2) | async-done | bytes 786464 | tf_op jit(solution)/shard_map/all_to_all | solution.py:179
  104.3 3.1 fusion.13
  108.3 2.1 fusion.16
  110.4 2.3 copy.94
  112.7 3.7 %reshape.446 = f32[768,512]{1,0:T(8,128)} reshape(f32[768,8,64]{2,1,0:T(8,128)} %bitcast.142) | data formatting | bytes 3145728
  116.5 1.4 reduce-scatter.7.cloned.1.call-done
  117.9 1.2 reshape.445
  120.1 5.5 %all-to-all-start.1 = ((bf16[8,64,192]{2,1,0:T(8,128)(2,1)}), bf16[8,64,192]{2,1,0:T(8,128)(2,1)S(1)}, u32[]{:S(2)}, u32[]{:S(2)}) async-start(bf16[8,64,192]{2,1,0:T(8,128)(2,1)} %copy.93), calls=%async_computation.1 | async-start | bytes 524288 | tf_op jit(solution)/shard_map/all_to_all | solution.py:154
  126.4 8.1 %all-to-all-done.1 = bf16[8,64,192]{2,1,0:T(8,128)(2,1)S(1)} async-done(((bf16[8,64,192]{2,1,0:T(8,128)(2,1)}), bf16[8,64,192]{2,1,0:T(8,128)(2,1)S(1)}, u32[]{:S(2)}, u32[]{:S(2)}) %all-to-all-start.1) | async-done | bytes 196640 | tf_op jit(solution)/shard_map/all_to_all | solution.py:154
  134.8 20.2 %all_gather.6 = bf16[8,64,768]{1,0,2:T(8,128)(2,1)} all-gather(bf16[8,64,192]{1,0,2:T(8,128)(2,1)S(1)} %copy.77), channel_id=1, replica_groups=mesh['ex'=8,'tp'=4] {'tp'}, dimensions={2}, use_global_device_ids=true | all-gather | bytes 983040 | tf_op jit(solution)/shard_map/all_gather | solution.py:160
  154.9 2.0 copy.78
  157.0 1.2 gather_fusion.1
  158.6 2.4 multiply_reduce_fusion
  161.0 1.2 reshape.447
  163.3 3.4 all-to-all-start.3
  166.8 9.5 %all-to-all-done.3 = bf16[8,64,192]{2,1,0:T(8,128)(2,1)S(1)} async-done(((bf16[8,64,192]{2,1,0:T(8,128)(2,1)}), bf16[8,64,192]{2,1,0:T(8,128)(2,1)S(1)}, u32[]{:S(2)}, u32[]{:S(2)}) %all-to-all-start.3) | async-done | bytes 196640 | tf_op jit(solution)/shard_map/all_to_all | solution.py:198
  176.6 13.6 %all_gather.7 = bf16[8,64,768]{1,0,2:T(8,128)(2,1)} all-gather(bf16[8,64,192]{1,0,2:T(8,128)(2,1)S(1)} %copy.82), channel_id=1, replica_groups=mesh['ex'=8,'tp'=4] {'tp'}, dimensions={2}, use_global_device_ids=true | all-gather | bytes 983040 | tf_op jit(solution)/shard_map/all_gather | solution.py:199
  190.2 2.0 copy.83
  192.2 1.9 gather_fusion.3
  194.1 1.4 reshape.395
  195.5 1.7 reduce_sum.177
  197.3 1.5 multiply_reduce_fusion.2
  201.0 1.1 fusion.84
  205.6 1.1 fusion.88
  206.7 3.5 convolution_bitcast_fusion.1
  210.2 3.5 convolution_bitcast_fusion
  215.2 21.0 %all-reduce.10.cloned.1.call-done = bf16[128,768]{1,0:T(8,128)(2,1)} async-done(((bf16[128,768]{1,0:T(8,128)(2,1)}), bf16[128,768]{1,0:T(8,128)(2,1)}) %all-reduce.10.cloned.1.call-update) | async-done | bytes 196624 | tf_op jit(solution)/shard_map/psum | solution.py:254
  236.2 1.2 fusion.40
  237.4 40.2 %all-reduce.2 = (f32[768]{0:T(1024)}, f32[768]{0:T(1024)}, f32[32,3]{0,1:T(4,128)}, f32[768,8]{0,1:T(8,128)}) all-reduce(f32[768]{0:T(1024)S(1)} %get-tuple-element.16, f32[768]{0:T(1024)S(1)} %get-tuple-element.12, f32[32,3]{0,1:T(4,128)S(1)} %fusion.25, f32[768,8]{0,1:T(8,128)S(1)} %fusion.97), channel_id=1, replica_groups=mesh['ex'=8,'tp'=4] {'ex'}, use_global_device_ids=true, to_apply=%region_28.29 | all-reduce | flops 7776 | bytes 62208 | tf_op jit(solution)/shard_map/psum | solution.py:262
  277.6 1.8 fusion.37
  279.4 72.0 %all-reduce.12.cloned.1.call-done = (f32[768,192]{0,1:T(8,128)}, f32[768,192]{0,1:T(8,128)}, f32[768,192]{0,1:T(8,128)}, f32[192,768]{1,0:T(8,128)}) async-done(((f32[768,192]{0,1:T(8,128)}, f32[768,192]{0,1:T(8,128)}, f32[768,192]{0,1:T(8,128)}, f32[192,768]{1,0:T(8,128)}), (f32[768,192]{0,1:T(8,128)}, f32[768,192]{0,1:T(8,128)}, f32[768,192]{0,1:T(8,128)}, ...) | async-done | bytes 2359312 | tf_op jit(solution)/shard_map/psum | solution.py:262
  351.4 2.0 copy.102
  (178 shorter events, 24.4 us)
Async XLA Ops:
  7.2 80.7 %copy-start = (bf16[1,768,768]{2,1,0:T(8,128)(2,1)S(1)}, bf16[1,768,768]{2,1,0:T(8,128)(2,1)}, u32[]{:S(2)}) copy-start(bf16[1,768,768]{2,1,0:T(8,128)(2,1)} %param.26) | copy-start | bytes 3538948
  7.2 4.5 %copy-start.1 = (bf16[128,768]{1,0:T(8,128)(2,1)S(1)}, bf16[128,768]{1,0:T(8,128)(2,1)}, u32[]{:S(2)}) copy-start(bf16[128,768]{1,0:T(8,128)(2,1)} %param.14) | copy-start | bytes 589828
  7.2 4.5 %copy-start.26 = (f32[768]{0:T(1024)S(1)}, f32[768]{0:T(1024)}, u32[]{:S(2)}) copy-start(f32[768]{0:T(1024)} %param.21) | copy-start | bytes 9220
  7.2 4.5 %copy-start.16 = (bf16[768,192]{0,1:T(8,128)(2,1)S(1)}, bf16[768,192]{0,1:T(8,128)(2,1)}, u32[]{:S(2)}) copy-start(bf16[768,192]{0,1:T(8,128)(2,1)} %param.17) | copy-start | bytes 884740
  7.2 4.8 %copy-start.18 = (bf16[768,192]{0,1:T(8,128)(2,1)S(1)}, bf16[768,192]{0,1:T(8,128)(2,1)}, u32[]{:S(2)}) copy-start(bf16[768,192]{0,1:T(8,128)(2,1)} %param.18) | copy-start | bytes 884740
  7.2 5.1 %copy-start.45 = (s32[1,4]{1,0:T(1,128)S(1)}, s32[1,4]{1,0:T(1,128)}, u32[]{:S(2)}) copy-start(s32[1,4]{1,0:T(1,128)} %param.16) | copy-start | bytes 52
  7.3 43.1 %all-reduce.8.cloned.1.call-start = ((), (), s32[]{:S(2)}) async-start(), calls=%async_computation.6 | async-start | bytes 786432 | tf_op jit(solution)/shard_map/psum | solution.py:115
  7.4 5.3 %copy-start.27 = (s32[128,128]{1,0:T(8,128)}, s32[128,128]{1,0:T(8,128)S(1)}, u32[]{:S(2)}) copy-start(s32[128,128]{1,0:T(8,128)S(1)} %compare_select_fusion) | copy-start | bytes 196612
  8.7 4.0 %copy-start.35 = (f32[128]{0:T(128)}, f32[128]{0:T(128)S(1)}, u32[]{:S(2)}) copy-start(f32[128]{0:T(128)S(1)} %add_rsqrt_fusion.1) | copy-start | bytes 1540
  10.1 3.8 %copy-start.6 = (bf16[192,768]{1,0:T(8,128)(2,1)S(1)}, bf16[192,768]{1,0:T(8,128)(2,1)}, u32[]{:S(2)}) copy-start(bf16[192,768]{1,0:T(8,128)(2,1)} %param.20) | copy-start | bytes 884740
  11.7 1.4 copy-start.24
  11.7 3.2 copy-start.31
  12.4 39.1 %copy-start.22 = (bf16[128,192]{0,1:T(8,128)(2,1)}, bf16[128,192]{0,1:T(8,128)(2,1)S(1)}, u32[]{:S(2)}) copy-start(bf16[128,192]{0,1:T(8,128)(2,1)S(1)} %convolution_convert_fusion.4) | copy-start | bytes 147460
  13.0 39.0 %copy-start.30 = (f32[768]{0:T(1024)S(1)}, f32[768]{0:T(1024)}, u32[]{:S(2)}) copy-start(f32[768]{0:T(1024)} %param.22) | copy-start | bytes 9220
  15.6 2.0 copy-start.42
  55.5 5.6 %copy-start.4 = (bf16[128,768]{1,0:T(8,128)(2,1)S(1)}, bf16[128,768]{1,0:T(8,128)(2,1)}, u32[]{:S(2)}) copy-start(bf16[128,768]{1,0:T(8,128)(2,1)} %param.27) | copy-start | bytes 589828
  55.5 24.9 %all-to-all-start = ((bf16[8,64,768]{2,1,0:T(8,128)(2,1)}), bf16[8,64,768]{2,1,0:T(8,128)(2,1)}, u32[]{:S(2)}, u32[]{:S(2)}) async-start(bf16[8,64,768]{2,1,0:T(8,128)(2,1)} %bitcast.10), calls=%async_computation | async-start | bytes 1572864 | tf_op jit(solution)/shard_map/all_to_all | solution.py:144
  61.9 3.4 copy-start.37
  65.0 3.0 copy-start.11
  80.4 4.4 %copy-start.44 = (bf16[1,768,768]{2,1,0:T(8,128)(2,1)S(1)}, bf16[1,768,768]{2,1,0:T(8,128)(2,1)}, u32[]{:S(2)}) copy-start(bf16[1,768,768]{2,1,0:T(8,128)(2,1)} %param.25) | copy-start | bytes 3538948
  80.4 23.9 %all-to-all-start.2 = ((bf16[8,64,768]{2,1,0:T(8,128)(2,1)}), bf16[8,64,768]{2,1,0:T(8,128)(2,1)}, u32[]{:S(2)}, u32[]{:S(2)}) async-start(bf16[8,64,768]{2,1,0:T(8,128)(2,1)} %bitcast.22), calls=%async_computation.2 | async-start | bytes 1572864 | tf_op jit(solution)/shard_map/all_to_all | solution.py:179
  84.8 33.1 %reduce-scatter.7.cloned.1.call-start = ((), (), s32[]{:S(2)}) async-start(), calls=%async_computation.8 | async-start | bytes 983040
  93.6 67.4 %reduce-scatter.9.cloned.1.call-start = ((), (), s32[]{:S(2)}) async-start(), calls=%async_computation.9 | async-start | bytes 1966080
  116.4 9.2 %copy-start.5 = (bf16[128,768]{1,0:T(8,128)(2,1)S(1)}, bf16[128,768]{1,0:T(8,128)(2,1)}, u32[]{:S(2)}) copy-start(bf16[128,768]{1,0:T(8,128)(2,1)} %param.27) | copy-start | bytes 589828
  116.5 9.9 %copy-start.43 = (s32[256,1]{0,1:T(1,128)S(1)}, s32[256,1]{0,1:T(1,128)}, u32[]{:S(2)}) copy-start(s32[256,1]{0,1:T(1,128)} %copy-done.42) | copy-start | bytes 3076
  120.1 14.4 %all-to-all-start.1 = ((bf16[8,64,192]{2,1,0:T(8,128)(2,1)}), bf16[8,64,192]{2,1,0:T(8,128)(2,1)S(1)}, u32[]{:S(2)}, u32[]{:S(2)}) async-start(bf16[8,64,192]{2,1,0:T(8,128)(2,1)} %copy.93), calls=%async_computation.1 | async-start | bytes 524288 | tf_op jit(solution)/shard_map/all_to_all | solution.py:154
  156.9 1.6 copy-start.12
  158.5 8.2 %copy-start.34 = (f32[128]{0:T(128)S(1)}, f32[128]{0:T(128)}, u32[]{:S(2)}) copy-start(f32[128]{0:T(128)} %copy-done.33) | copy-start | bytes 1540
  158.6 8.2 %copy-start.39 = (f32[128]{0:T(128)S(1)}, f32[128]{0:T(128)}, u32[]{:S(2)}) copy-start(f32[128]{0:T(128)} %copy-done.38) | copy-start | bytes 1540
  158.6 8.2 %copy-start.32 = (s32[128,2]{0,1:T(2,128)S(1)}, s32[128,2]{0,1:T(2,128)}, u32[]{:S(2)}) copy-start(s32[128,2]{0,1:T(2,128)} %param.15) | copy-start | bytes 3076
  163.3 13.1 %all-to-all-start.3 = ((bf16[8,64,192]{2,1,0:T(8,128)(2,1)}), bf16[8,64,192]{2,1,0:T(8,128)(2,1)S(1)}, u32[]{:S(2)}, u32[]{:S(2)}) async-start(bf16[8,64,192]{2,1,0:T(8,128)(2,1)} %copy.95), calls=%async_computation.3 | async-start | bytes 524288 | tf_op jit(solution)/shard_map/all_to_all | solution.py:198
  166.7 69.5 %all-reduce.10.cloned.1.call-start = ((), (), s32[]{:S(2)}) async-start(), calls=%async_computation.7 | async-start | bytes 393216 | tf_op jit(solution)/shard_map/psum | solution.py:254
  194.1 3.1 copy-start.29
  194.1 3.1 copy-start.41
  197.3 2.4 copy-start.7
  198.8 1.4 copy-start.23
  198.9 1.5 copy-start.21
  199.6 1.4 copy-start.36
  200.1 2.0 copy-start.14
  200.8 3.5 copy-start.19
  202.2 2.4 copy-start.15
  205.5 145.8 %all-reduce.12.cloned.1.call-start = ((), (), s32[]{:S(2)}) async-start(), calls=%async_computation.10 | async-start | bytes 4718592 | tf_op jit(solution)/shard_map/psum | solution.py:262
  206.7 3.5 copy-start.47
  210.2 3.5 copy-start.3
  210.2 3.9 %copy-start.28 = (s32[128,128]{1,0:T(8,128)S(1)}, s32[128,128]{1,0:T(8,128)}, u32[]{:S(2)}) copy-start(s32[128,128]{1,0:T(8,128)} %copy-done.27) | copy-start | bytes 196612
  351.4 2.1 copy-start.10
  351.4 2.9 copy-start.9
  351.4 3.7 %copy-start.8 = (f32[192,768]{1,0:T(8,128)S(1)}, f32[192,768]{1,0:T(8,128)}, u32[]{:S(2)}) copy-start(f32[192,768]{1,0:T(8,128)} %get-tuple-element.44) | copy-start | bytes 1769476
  (11 other events, 9.4 us)
Sparse Core Ops, SparseCore 0:
  15.0 35.3 all-reduce.7
  93.7 24.1 reduce-scatter.6
  121.0 34.1 reduce-scatter.8
  205.6 30.4 all-reduce.9
  240.5 110.7 all-reduce.11
where the time goes:
time: 364 us; the launch traced here: 362 us
  waiting for transfers between devices  168 us (46%)
  blocking collectives  74 us (20%)
  local copies, waits for them, and re-layouts  41.8 us (11%)
  matrix products  31.6 us (9%)
  starting transfers between devices  19.3 us (5%)
  between operations  14.6 us (4%)
  other arithmetic  13.4 us (4%)
    psum x1, waiting for transfers between devices, shards(): lax.psum((grad_w_query, grad_w_key, grad_w_value, grad_w_attn_out, grad_g...  72 us
    psum x1, blocking collectives, shards(): lax.psum((grad_w_query, grad_w_key, grad_w_value, grad_w_attn_out, grad_g...  40.2 us
    psum x1, waiting for transfers between devices, shards(): residual = inputs_f + lax.psum(head_part, 'tp')  32.7 us
    unnamed x113, local copies, waits for them, and re-layouts  23.8 us
    psum x1, waiting for transfers between devices, shards(): lax.psum(input_part.astype(jnp.bfloat16), 'tp').astype(jnp.float32)  21 us
    all_gather x1, blocking collectives, shards(): lax.all_gather(returned, 'tp', axis=2, tiled=True)  20.2 us
    all_gather x1, blocking collectives, shards(): lax.all_gather(row_back, 'tp', axis=2, tiled=True)  13.6 us
    all_to_all x1, waiting for transfers between devices, shards(): lax.all_to_all(send_rows, 'ex', split_axis=0, concat_axis=0, tiled=True)  12.4 us
  transfers between devices with their start and end apart: 9, of which 8 were waited for; matrix products, arithmetic and copies ran while one was open for 14% of the time, Pallas kernels for 0%

commit v1 on v0

--- a/solution.py
+++ b/solution.py
@@ -251,7 +251,9 @@
         + contract_cols(key_grad, w_key)
         + contract_cols(value_flat, w_value)
     )
-    input_grad = lax.psum(input_part.astype(jnp.bfloat16), "tp").astype(jnp.float32)
+    input_grad = jnp.sum(lax.all_gather(input_part.astype(jnp.bfloat16), "tp"), axis=0).astype(
+        jnp.float32
+    )
     grad_gain_attn = jnp.sum(input_grad * normed_a, 0)
     normed_grad_a = input_grad * gain_attn
     grad_inputs = (

time: 364 us -> 328 us (0.901)
  waiting for transfers between devices: 168 us -> 126 us
  blocking collectives: 74 us -> 80.6 us
    psum x1 -> x0, waiting for transfers between devices: 21 us -> none  [shards(): lax.psum(input_part.astype(jnp.bfloat16), 'tp').astype(jnp.float32)]
    psum x1, waiting for transfers between devices: 72 us -> 56.1 us  [shards(): lax.psum((grad_w_query, grad_w_key, grad_w_value, grad_w_attn_out, grad_g...]
    all_gather x0 -> x1, blocking collectives: none -> 8.74 us  [shards(): lax.all_gather(input_part.astype(jnp.bfloat16), 'tp')]
    unnamed x113 -> x109, local copies, waits for them, and re-layouts: 23.8 us -> 25.2 us
  transfers between devices with their start and end apart: 9 -> 8, of which waited for: 8 -> 6; matrix products, arithmetic and copies ran while one was open for 14% -> 15% of each run, Pallas kernels for 0% -> 0%
where the time goes in v1:
time: 328 us; the launch traced here: 327 us
  waiting for transfers between devices  126 us (38%)
  blocking collectives  80.6 us (25%)
  local copies, waits for them, and re-layouts  43.2 us (13%)
  matrix products  31.5 us (10%)
  starting transfers between devices  18.9 us (6%)
  between operations  14.6 us (4%)
  other arithmetic  11.7 us (4%)
    psum x1, waiting for transfers between devices, shards(): lax.psum((grad_w_query, grad_w_key, grad_w_value, grad_w_attn_out, grad_g...  56.1 us
    psum x1, blocking collectives, shards(): lax.psum((grad_w_query, grad_w_key, grad_w_value, grad_w_attn_out, grad_g...  37.5 us
    psum x1, waiting for transfers between devices, shards(): residual = inputs_f + lax.psum(head_part, 'tp')  32.7 us
    unnamed x109, local copies, waits for them, and re-layouts  25.2 us
    all_gather x1, blocking collectives, shards(): lax.all_gather(returned, 'tp', axis=2, tiled=True)  20.7 us
    all_gather x1, blocking collectives, shards(): lax.all_gather(row_back, 'tp', axis=2, tiled=True)  13.7 us
    all_to_all x1, waiting for transfers between devices, shards(): lax.all_to_all(send_rows, 'ex', split_axis=0, concat_axis=0, tiled=True)  12.4 us
    all_to_all x1, waiting for transfers between devices, shards(): lax.all_to_all(send_grad_rows, 'ex', split_axis=0, concat_axis=0, tiled=T...  10.5 us
  transfers between devices with their start and end apart: 8, of which 6 were waited for; matrix products, arithmetic and copies ran while one was open for 15% of the time, Pallas kernels for 0%

profile of v1, /device:TPU:0, one launch (start us, length us, event | category | flops | bytes accessed | tf_op | source)
XLA Modules:
  0.0 326.7 jit_solution(12547431043709358117)
XLA Ops:
  7.4 1.2 fusion.41
  8.7 1.4 fusion.1
  10.3 1.4 convolution_convert_fusion.6
  15.6 1.4 scatter_custom_fusion
  17.6 32.7 %all-reduce.7.cloned.1.call-done = f32[128,768]{1,0:T(8,128)} async-done(((f32[128,768]{1,0:T(8,128)}), f32[128,768]{1,0:T(8,128)}) %all-reduce.7.cloned.1.call-update) | async-done | bytes 393232 | tf_op jit(solution)/shard_map/psum | solution.py:115
  50.4 1.1 multiply_reduce_fusion.4
  52.8 2.7 gather_fusion
  55.5 5.6 %all-to-all-start = ((bf16[8,64,768]{2,1,0:T(8,128)(2,1)}), bf16[8,64,768]{2,1,0:T(8,128)(2,1)}, u32[]{:S(2)}, u32[]{:S(2)}) async-start(bf16[8,64,768]{2,1,0:T(8,128)(2,1)} %bitcast.10), calls=%async_computation | async-start | bytes 1572864 | tf_op jit(solution)/shard_map/all_to_all | solution.py:144
  65.3 2.7 gather_fusion.2
  68.1 12.4 %all-to-all-done = bf16[8,64,768]{2,1,0:T(8,128)(2,1)} async-done(((bf16[8,64,768]{2,1,0:T(8,128)(2,1)}), bf16[8,64,768]{2,1,0:T(8,128)(2,1)}, u32[]{:S(2)}, u32[]{:S(2)}) %all-to-all-start) | async-done | bytes 786464 | tf_op jit(solution)/shard_map/all_to_all | solution.py:144
  80.4 4.3 %all-to-all-start.2 = ((bf16[8,64,768]{2,1,0:T(8,128)(2,1)}), bf16[8,64,768]{2,1,0:T(8,128)(2,1)}, u32[]{:S(2)}, u32[]{:S(2)}) async-start(bf16[8,64,768]{2,1,0:T(8,128)(2,1)} %bitcast.22), calls=%async_computation.2 | async-start | bytes 1572864 | tf_op jit(solution)/shard_map/all_to_all | solution.py:179
  84.8 1.9 fusion.18
  86.8 1.1 copy-done.46
  87.9 1.9 convolution_convert_fusion
  89.9 2.0 copy.92
  91.9 1.7 reshape.445
  93.8 10.5 %all-to-all-done.2 = bf16[8,64,768]{2,1,0:T(8,128)(2,1)} async-done(((bf16[8,64,768]{2,1,0:T(8,128)(2,1)}), bf16[8,64,768]{2,1,0:T(8,128)(2,1)}, u32[]{:S(2)}, u32[]{:S(2)}) %all-to-all-start.2) | async-done | bytes 786464 | tf_op jit(solution)/shard_map/all_to_all | solution.py:179
  104.3 3.1 fusion.13
  108.4 2.1 fusion.16
  110.5 2.3 copy.94
  112.8 3.7 %reshape.447 = f32[768,512]{1,0:T(8,128)} reshape(f32[768,8,64]{2,1,0:T(8,128)} %bitcast.143) | data formatting | bytes 3145728
  118.2 1.2 reshape.446
  120.4 5.2 %all-to-all-start.1 = ((bf16[8,64,192]{2,1,0:T(8,128)(2,1)}), bf16[8,64,192]{2,1,0:T(8,128)(2,1)S(1)}, u32[]{:S(2)}, u32[]{:S(2)}) async-start(bf16[8,64,192]{2,1,0:T(8,128)(2,1)} %copy.93), calls=%async_computation.1 | async-start | bytes 524288 | tf_op jit(solution)/shard_map/all_to_all | solution.py:154
  125.6 4.0 %convolution_bitcast_fusion = f32[1,768,768]{2,1,0:T(8,128)} fusion(bf16[8,64,768]{2,1,0:T(8,128)(2,1)} %all-to-all-done.2, f32[8,64,768]{2,1,0:T(8,128)} %copy-done.46), kind=kOutput, calls=%fused_computation.10 | convolution fusion | flops 607518720 | bytes 4718592 | tf_op jit(solution)/shard_map/slcf,slcd->lfd/dot_general | solution.py:186
  129.5 5.0 %all-to-all-done.1 = bf16[8,64,192]{2,1,0:T(8,128)(2,1)S(1)} async-done(((bf16[8,64,192]{2,1,0:T(8,128)(2,1)}), bf16[8,64,192]{2,1,0:T(8,128)(2,1)S(1)}, u32[]{:S(2)}, u32[]{:S(2)}) %all-to-all-start.1) | async-done | bytes 196640 | tf_op jit(solution)/shard_map/all_to_all | solution.py:154
  134.7 20.7 %all_gather.12 = bf16[8,64,768]{1,0,2:T(8,128)(2,1)} all-gather(bf16[8,64,192]{1,0,2:T(8,128)(2,1)S(1)} %copy.77), channel_id=1, replica_groups=mesh['ex'=8,'tp'=4] {'tp'}, dimensions={2}, use_global_device_ids=true | all-gather | bytes 983040 | tf_op jit(solution)/shard_map/all_gather | solution.py:160
  155.4 2.0 copy.78
  157.4 1.2 gather_fusion.1
  159.1 2.4 multiply_reduce_fusion
  161.5 1.2 reshape.448
  163.7 3.4 %all-to-all-start.3 = ((bf16[8,64,192]{2,1,0:T(8,128)(2,1)}), bf16[8,64,192]{2,1,0:T(8,128)(2,1)S(1)}, u32[]{:S(2)}, u32[]{:S(2)}) async-start(bf16[8,64,192]{2,1,0:T(8,128)(2,1)} %copy.95), calls=%async_computation.3 | async-start | bytes 524288 | tf_op jit(solution)/shard_map/all_to_all | solution.py:198
  167.3 9.5 %all-to-all-done.3 = bf16[8,64,192]{2,1,0:T(8,128)(2,1)S(1)} async-done(((bf16[8,64,192]{2,1,0:T(8,128)(2,1)}), bf16[8,64,192]{2,1,0:T(8,128)(2,1)S(1)}, u32[]{:S(2)}, u32[]{:S(2)}) %all-to-all-start.3) | async-done | bytes 196640 | tf_op jit(solution)/shard_map/all_to_all | solution.py:198
  177.1 13.7 %all_gather.13 = bf16[8,64,768]{1,0,2:T(8,128)(2,1)} all-gather(bf16[8,64,192]{1,0,2:T(8,128)(2,1)S(1)} %copy.82), channel_id=1, replica_groups=mesh['ex'=8,'tp'=4] {'tp'}, dimensions={2}, use_global_device_ids=true | all-gather | bytes 983040 | tf_op jit(solution)/shard_map/all_gather | solution.py:199
  190.7 2.0 copy.83
  192.8 1.9 gather_fusion.3
  194.7 1.4 reshape.395
  196.1 1.7 reduce_sum.189
  197.8 1.5 multiply_reduce_fusion.2
  201.3 1.1 fusion.46
  202.4 1.1 fusion.84
  203.5 1.1 fusion.86
  204.6 1.1 fusion.88
  205.8 3.6 %convolution_bitcast_fusion.1 = f32[1,768,768]{2,1,0:T(8,128)} fusion(bf16[8,64,768]{2,1,0:T(8,128)(2,1)} %all-to-all-done, bf16[8,64,768]{2,1,0:T(8,128)(2,1)} %copy-done.47), kind=kOutput, calls=%fused_computation.11 | convolution fusion | flops 603979776 | bytes 3932160 | tf_op jit(solution)/shard_map/slcd,slcf->ldf/dot_general | solution.py:190
  211.0 8.7 %all-gather = bf16[512,768]{1,0:T(8,128)(2,1)S(1)} all-gather(bf16[128,768]{1,0:T(8,128)(2,1)S(1)} %fusion.20), channel_id=2, replica_groups=mesh['ex'=8,'tp'=4] {'tp'}, dimensions={0}, use_global_device_ids=true | all-gather | bytes 983040 | tf_op jit(solution)/shard_map/all_gather | solution.py:254
  219.8 1.1 fusion.25
  221.2 37.5 %all-reduce.2 = (f32[768]{0:T(1024)}, f32[768]{0:T(1024)}, f32[32,3]{0,1:T(4,128)}, f32[768,8]{0,1:T(8,128)}) all-reduce(f32[768]{0:T(1024)S(1)} %get-tuple-element.16, f32[768]{0:T(1024)S(1)} %get-tuple-element.12, f32[32,3]{0,1:T(4,128)S(1)} %fusion.25, f32[768,8]{0,1:T(8,128)S(1)} %fusion.97), channel_id=1, replica_groups=mesh['ex'=8,'tp'=4] {'ex'}, use_global_device_ids=true, to_apply=%region_28.29 | all-reduce | flops 7776 | bytes 62208 | tf_op jit(solution)/shard_map/psum | solution.py:264
  259.5 56.1 %all-reduce.9.cloned.1.call-done = (f32[768,192]{0,1:T(8,128)}, f32[768,192]{0,1:T(8,128)}, f32[768,192]{0,1:T(8,128)}, f32[192,768]{1,0:T(8,128)}) async-done(((f32[768,192]{0,1:T(8,128)}, f32[768,192]{0,1:T(8,128)}, f32[768,192]{0,1:T(8,128)}, f32[192,768]{1,0:T(8,128)}), (f32[768,192]{0,1:T(8,128)}, f32[768,192]{0,1:T(8,128)}, f32[768,192]{0,1:T(8,128)}, ...) | async-done | bytes 2359312 | tf_op jit(solution)/shard_map/psum | solution.py:264
  315.7 2.0 copy.101
  (173 shorter events, 23.1 us)
Async XLA Ops:
  7.2 80.7 %copy-start = (bf16[1,768,768]{2,1,0:T(8,128)(2,1)S(1)}, bf16[1,768,768]{2,1,0:T(8,128)(2,1)}, u32[]{:S(2)}) copy-start(bf16[1,768,768]{2,1,0:T(8,128)(2,1)} %param.26) | copy-start | bytes 3538948
  7.2 4.5 %copy-start.1 = (bf16[128,768]{1,0:T(8,128)(2,1)S(1)}, bf16[128,768]{1,0:T(8,128)(2,1)}, u32[]{:S(2)}) copy-start(bf16[128,768]{1,0:T(8,128)(2,1)} %param.14) | copy-start | bytes 589828
  7.2 4.5 %copy-start.26 = (f32[768]{0:T(1024)S(1)}, f32[768]{0:T(1024)}, u32[]{:S(2)}) copy-start(f32[768]{0:T(1024)} %param.21) | copy-start | bytes 9220
  7.2 4.5 %copy-start.16 = (bf16[768,192]{0,1:T(8,128)(2,1)S(1)}, bf16[768,192]{0,1:T(8,128)(2,1)}, u32[]{:S(2)}) copy-start(bf16[768,192]{0,1:T(8,128)(2,1)} %param.17) | copy-start | bytes 884740
  7.2 4.8 %copy-start.18 = (bf16[768,192]{0,1:T(8,128)(2,1)S(1)}, bf16[768,192]{0,1:T(8,128)(2,1)}, u32[]{:S(2)}) copy-start(bf16[768,192]{0,1:T(8,128)(2,1)} %param.18) | copy-start | bytes 884740
  7.2 5.1 %copy-start.45 = (s32[1,4]{1,0:T(1,128)S(1)}, s32[1,4]{1,0:T(1,128)}, u32[]{:S(2)}) copy-start(s32[1,4]{1,0:T(1,128)} %param.16) | copy-start | bytes 52
  7.3 43.1 %all-reduce.7.cloned.1.call-start = ((), (), s32[]{:S(2)}) async-start(), calls=%async_computation.6 | async-start | bytes 786432 | tf_op jit(solution)/shard_map/psum | solution.py:115
  7.4 5.3 %copy-start.27 = (s32[128,128]{1,0:T(8,128)}, s32[128,128]{1,0:T(8,128)S(1)}, u32[]{:S(2)}) copy-start(s32[128,128]{1,0:T(8,128)S(1)} %compare_select_fusion) | copy-start | bytes 196612
  8.7 4.0 %copy-start.35 = (f32[128]{0:T(128)}, f32[128]{0:T(128)S(1)}, u32[]{:S(2)}) copy-start(f32[128]{0:T(128)S(1)} %add_rsqrt_fusion.1) | copy-start | bytes 1540
  10.1 3.8 %copy-start.6 = (bf16[192,768]{1,0:T(8,128)(2,1)S(1)}, bf16[192,768]{1,0:T(8,128)(2,1)}, u32[]{:S(2)}) copy-start(bf16[192,768]{1,0:T(8,128)(2,1)} %param.20) | copy-start | bytes 884740
  11.7 1.4 copy-start.24
  11.7 3.2 copy-start.31
  12.4 39.1 %copy-start.22 = (bf16[128,192]{0,1:T(8,128)(2,1)}, bf16[128,192]{0,1:T(8,128)(2,1)S(1)}, u32[]{:S(2)}) copy-start(bf16[128,192]{0,1:T(8,128)(2,1)S(1)} %convolution_convert_fusion.4) | copy-start | bytes 147460
  13.0 39.0 %copy-start.30 = (f32[768]{0:T(1024)S(1)}, f32[768]{0:T(1024)}, u32[]{:S(2)}) copy-start(f32[768]{0:T(1024)} %param.22) | copy-start | bytes 9220
  15.6 2.0 copy-start.42
  55.5 5.6 %copy-start.4 = (bf16[128,768]{1,0:T(8,128)(2,1)S(1)}, bf16[128,768]{1,0:T(8,128)(2,1)}, u32[]{:S(2)}) copy-start(bf16[128,768]{1,0:T(8,128)(2,1)} %param.27) | copy-start | bytes 589828
  55.5 24.9 %all-to-all-start = ((bf16[8,64,768]{2,1,0:T(8,128)(2,1)}), bf16[8,64,768]{2,1,0:T(8,128)(2,1)}, u32[]{:S(2)}, u32[]{:S(2)}) async-start(bf16[8,64,768]{2,1,0:T(8,128)(2,1)} %bitcast.10), calls=%async_computation | async-start | bytes 1572864 | tf_op jit(solution)/shard_map/all_to_all | solution.py:144
  61.9 3.4 %copy-start.37 = (s32[1024]{0:T(1024)S(1)}, s32[1024]{0:T(1024)}, u32[]{:S(2)}) copy-start(s32[1024]{0:T(1024)} %get-tuple-element.37) | copy-start | bytes 12292
  65.0 3.0 copy-start.11
  80.4 4.4 %copy-start.44 = (bf16[1,768,768]{2,1,0:T(8,128)(2,1)S(1)}, bf16[1,768,768]{2,1,0:T(8,128)(2,1)}, u32[]{:S(2)}) copy-start(bf16[1,768,768]{2,1,0:T(8,128)(2,1)} %param.25) | copy-start | bytes 3538948
  80.4 23.9 %all-to-all-start.2 = ((bf16[8,64,768]{2,1,0:T(8,128)(2,1)}), bf16[8,64,768]{2,1,0:T(8,128)(2,1)}, u32[]{:S(2)}, u32[]{:S(2)}) async-start(bf16[8,64,768]{2,1,0:T(8,128)(2,1)} %bitcast.22), calls=%async_computation.2 | async-start | bytes 1572864 | tf_op jit(solution)/shard_map/all_to_all | solution.py:179
  84.8 33.4 %reduce-scatter.7.cloned.1.call-start = ((), (), s32[]{:S(2)}) async-start(), calls=%async_computation.7 | async-start | bytes 983040
  86.8 1.1 copy-start.46
  93.6 67.9 %reduce-scatter.9.cloned.1.call-start = ((), (), s32[]{:S(2)}) async-start(), calls=%async_computation.8 | async-start | bytes 1966080
  116.5 1.7 copy-start.43
  120.4 14.1 %all-to-all-start.1 = ((bf16[8,64,192]{2,1,0:T(8,128)(2,1)}), bf16[8,64,192]{2,1,0:T(8,128)(2,1)S(1)}, u32[]{:S(2)}, u32[]{:S(2)}) async-start(bf16[8,64,192]{2,1,0:T(8,128)(2,1)} %copy.93), calls=%async_computation.1 | async-start | bytes 524288 | tf_op jit(solution)/shard_map/all_to_all | solution.py:154
  157.4 1.6 copy-start.12
  159.0 8.2 %copy-start.34 = (f32[128]{0:T(128)S(1)}, f32[128]{0:T(128)}, u32[]{:S(2)}) copy-start(f32[128]{0:T(128)} %copy-done.33) | copy-start | bytes 1540
  159.0 8.2 %copy-start.39 = (f32[128]{0:T(128)S(1)}, f32[128]{0:T(128)}, u32[]{:S(2)}) copy-start(f32[128]{0:T(128)} %copy-done.38) | copy-start | bytes 1540
  159.0 8.2 %copy-start.32 = (s32[128,2]{0,1:T(2,128)S(1)}, s32[128,2]{0,1:T(2,128)}, u32[]{:S(2)}) copy-start(s32[128,2]{0,1:T(2,128)} %param.15) | copy-start | bytes 3076
  163.7 13.1 %all-to-all-start.3 = ((bf16[8,64,192]{2,1,0:T(8,128)(2,1)}), bf16[8,64,192]{2,1,0:T(8,128)(2,1)S(1)}, u32[]{:S(2)}, u32[]{:S(2)}) async-start(bf16[8,64,192]{2,1,0:T(8,128)(2,1)} %copy.95), calls=%async_computation.3 | async-start | bytes 524288 | tf_op jit(solution)/shard_map/all_to_all | solution.py:198
  167.2 148.5 %all-reduce.9.cloned.1.call-start = ((), (), s32[]{:S(2)}) async-start(), calls=%async_computation.9 | async-start | bytes 4718592 | tf_op jit(solution)/shard_map/psum | solution.py:264
  194.7 3.1 copy-start.29
  194.7 3.1 copy-start.41
  197.8 2.4 copy-start.7
  199.4 1.1 copy-start.25
  199.4 1.4 copy-start.23
  199.4 1.5 copy-start.21
  200.2 1.1 copy-start.14
  200.4 2.0 copy-start.36
  205.8 3.7 %copy-start.3 = (bf16[128,768]{1,0:T(8,128)(2,1)S(1)}, bf16[128,768]{1,0:T(8,128)(2,1)}, u32[]{:S(2)}) copy-start(bf16[128,768]{1,0:T(8,128)(2,1)} %copy-done.2) | copy-start | bytes 589828
  205.8 4.0 %copy-start.17 = (bf16[768,192]{0,1:T(8,128)(2,1)S(1)}, bf16[768,192]{0,1:T(8,128)(2,1)}, u32[]{:S(2)}) copy-start(bf16[768,192]{0,1:T(8,128)(2,1)} %param.17) | copy-start | bytes 884740
  209.4 1.0 copy-start.19
  209.4 1.3 copy-start.15
  210.7 9.1 %copy-start.28 = (s32[128,128]{1,0:T(8,128)S(1)}, s32[128,128]{1,0:T(8,128)}, u32[]{:S(2)}) copy-start(s32[128,128]{1,0:T(8,128)} %copy-done.27) | copy-start | bytes 196612
  315.7 2.1 copy-start.10
  315.7 2.9 copy-start.9
  315.7 3.7 %copy-start.8 = (f32[192,768]{1,0:T(8,128)S(1)}, f32[192,768]{1,0:T(8,128)}, u32[]{:S(2)}) copy-start(f32[192,768]{1,0:T(8,128)} %get-tuple-element.44) | copy-start | bytes 1769476
  (8 other events, 5.8 us)
Sparse Core Ops, SparseCore 0:
  15.0 35.3 all-reduce.6
  93.7 24.1 reduce-scatter.6
  120.4 34.7 reduce-scatter.8
  205.9 109.7 all-reduce.8
